TPU v7x, 256 devices: a whole 4x4x8 slice. The times are simulated.
256 devices in a mesh: fsdp: 32 (over x, y, core), grp: 8 (over z).
Axes of the slice: x: 4, y: 4, z: 8, core: 2. Of those that a mesh axis runs over, the one named last changes fastest.
Arguments:
- grad: bfloat16 [16, 512, 7168], P(None, ('fsdp', 'grp')), may hold values from -6 to 6
- owner: int32 [224], replicated, may hold values from 0 to 511, as said below
- refresh: int32 [224], replicated, may hold values from 0 to 1, as said below
- stats_left: float32 [512, 512, 512], P(('fsdp', 'grp'))
- stats_right: float32 [512, 512, 512], P(('fsdp', 'grp'))
- old_roots: bfloat16 [512, 2, 512, 512], P(('fsdp', 'grp'))
- fresh_roots: bfloat16 [256, 2, 512, 512], P(('fsdp', 'grp'))
Outputs:
- new_left: float32 [512, 512, 512], P(('fsdp', 'grp'))
- new_right: float32 [512, 512, 512], P(('fsdp', 'grp'))
- update: bfloat16 [16, 512, 7168], P(None, ('fsdp', 'grp'))
Inputs may be any that keep to these rules, and one draw needn't show every extreme that they name: `owner`: no two blocks share a slot. Some device has all its 2 slots taken. `refresh`: of the blocks on one device at most one has 1; some block has 1.
All inputs are finite; a program needn't handle non-finite values.
Results may differ from a plain program's by a relative error of at most 0.0049.
Values may be sent and summed in bfloat16 or wider, within the bound.
A program may use at most 64 MiB of HBM per device.

v0:
```python
import jax
import jax.numpy as jnp
from jax import lax
from jax.sharding import PartitionSpec as P

decay_rate = 0.999
epsilon = 1e-06


def shifted(block, axis, distance):
    devices = range(lax.axis_size(axis))
    route = [((i - distance) % len(devices), i) for i in devices]
    return lax.ppermute(block, axis, route)


def slot_work(piece, left, right, inverse_roots):
    new_left = decay_rate * left + (1.0 - decay_rate) * jnp.dot(
        piece, piece.T, preferred_element_type=jnp.float32
    )
    new_right = decay_rate * right + (1.0 - decay_rate) * jnp.dot(
        piece.T, piece, preferred_element_type=jnp.float32
    )
    left_applied = jnp.dot(inverse_roots[0], piece, preferred_element_type=jnp.float32).astype(
        jnp.bfloat16
    )
    shaped = jnp.dot(left_applied, inverse_roots[1], preferred_element_type=jnp.float32)
    wide = piece.astype(jnp.float32)
    graft_scale = jnp.sqrt(jnp.mean(wide * wide) + epsilon) / jnp.sqrt(
        jnp.mean(shaped * shaped) + epsilon
    )
    return (new_left, new_right, (shaped * graft_scale).astype(jnp.bfloat16))


def local(grad, owner, refresh, stats_left, stats_right, old_roots, fresh_roots):
    matrices, row_count, width = grad.shape
    capacity, block_size = (stats_left.shape[0], stats_left.shape[1])
    block_cols = width // block_size
    fsdp_count = lax.axis_size("fsdp")
    grp_count = lax.axis_size("grp")
    device_total = fsdp_count * grp_count
    row_blocks = row_count * device_total // block_size
    block_total = matrices * row_blocks * block_cols
    self_index = lax.axis_index("fsdp") * grp_count + lax.axis_index("grp")
    my_row = self_index // (device_total // row_blocks)
    local_blocks = grad.reshape(matrices, row_count, block_cols, block_size).transpose(0, 2, 1, 3)
    local_blocks = local_blocks.reshape(matrices * block_cols, row_count, block_size)
    slot_ids = jnp.arange(capacity, dtype=jnp.int32)[:, None, None]
    fsdp_ids = jnp.arange(fsdp_count, dtype=jnp.int32)[None, :, None]
    grp_ids = jnp.arange(grp_count, dtype=jnp.int32)[None, None, :]
    slot_order = ((fsdp_ids * grp_count + grp_ids) * capacity + slot_ids).reshape(-1)
    block_ids = jnp.arange(block_total, dtype=jnp.int32)
    matches = owner[None, :] == slot_order[:, None]
    present = jnp.any(matches, axis=1)
    chosen_block = jnp.sum(jnp.where(matches, block_ids[None, :], 0), axis=1)
    chosen_row = chosen_block // block_cols % row_blocks
    local_index = chosen_block // (row_blocks * block_cols) * block_cols + chosen_block % block_cols
    sending = present & (chosen_row == my_row)
    outbound = jnp.where(
        sending[:, None, None], local_blocks[local_index], jnp.zeros((), jnp.bfloat16)
    )
    outbound = outbound.reshape(capacity, fsdp_count, grp_count, row_count, block_size)
    inbound = lax.all_to_all(
        lax.all_to_all(outbound, "fsdp", split_axis=1, concat_axis=1, tiled=True),
        "grp",
        split_axis=2,
        concat_axis=2,
        tiled=True,
    )
    own_slots = self_index * capacity + jnp.arange(capacity, dtype=jnp.int32)
    own_matches = owner[None, :] == own_slots[:, None]
    occupied = jnp.any(own_matches, axis=1)
    own_block = jnp.sum(jnp.where(own_matches, block_ids[None, :], 0), axis=1)
    own_row = own_block // block_cols % row_blocks
    row_pick = (jnp.arange(row_blocks, dtype=jnp.int32)[None, :] == own_row[:, None])[
        :, :, None, None
    ]
    stacked = inbound.reshape(capacity, row_blocks, block_size, block_size)
    pieces = jnp.sum(jnp.where(row_pick, stacked, jnp.zeros((), jnp.bfloat16)), axis=1)
    renewal = jnp.sum(jnp.where(own_matches, refresh[None, :], 0), axis=1) == 1
    renewed = shifted(fresh_roots, "grp", 1)[0]
    inverse_roots = jnp.where(renewal[:, None, None, None], renewed[None], old_roots)
    lefts, rights, slot_update = jax.vmap(slot_work)(pieces, stats_left, stats_right, inverse_roots)
    new_left = jnp.where(occupied[:, None, None], lefts, stats_left)
    new_right = jnp.where(occupied[:, None, None], rights, stats_right)
    placed = jnp.where(row_pick, slot_update[:, None], jnp.zeros((), jnp.bfloat16))
    outgoing = placed.reshape(capacity, fsdp_count, grp_count, row_count, block_size)
    returned = lax.all_to_all(
        lax.all_to_all(outgoing, "fsdp", split_axis=1, concat_axis=1, tiled=True),
        "grp",
        split_axis=2,
        concat_axis=2,
        tiled=True,
    )
    returned = returned.reshape(capacity * device_total, row_count, block_size)
    matrix_ids = jnp.arange(matrices, dtype=jnp.int32)[:, None]
    column_ids = jnp.arange(block_cols, dtype=jnp.int32)[None, :]
    wanted = ((matrix_ids * row_blocks + my_row) * block_cols + column_ids).reshape(-1)
    wanted_owner = owner[wanted]
    position = wanted_owner % capacity * device_total + wanted_owner // capacity
    gathered = returned[position].reshape(matrices, block_cols, row_count, block_size)
    update = gathered.transpose(0, 2, 1, 3).reshape(matrices, row_count, width)
    return (new_left, new_right, update)


def solution(mesh):
    return jax.shard_map(
        local,
        mesh=mesh,
        in_specs=(
            P(None, ("fsdp", "grp"), None),
            P(),
            P(),
            P(("fsdp", "grp"), None, None),
            P(("fsdp", "grp"), None, None),
            P(("fsdp", "grp"), None, None, None),
            P(("fsdp", "grp"), None, None, None),
        ),
        out_specs=(
            P(("fsdp", "grp"), None, None),
            P(("fsdp", "grp"), None, None),
            P(None, ("fsdp", "grp"), None),
        ),
        check_vma=False,
    )
```

profile of v0, /device:TPU:1, one launch (start us, length us, event | category | flops | bytes accessed | tf_op | source)
XLA Modules:
  0.0 167.9 jit_solution(10023393125564104230)
XLA Ops:
  0.6 0.1 add_multiply_fusion
  0.7 0.1 add.230
  0.8 0.8 compare_reduce_fusion
  1.6 0.8 fusion.1
  2.6 0.1 and.88
  2.7 1.3 reshape.329
  4.0 0.5 copy.60
  4.5 3.6 %gather_fusion = bf16[512,2,512]{2,1,0:T(2,128)(2,1)S(1)} fusion(bf16[224,2,512]{2,1,0:T(2,128)(2,1)S(1)} %bitcast.33, s32[1024]{0:T(1024)S(1)} %pad_clamp_fusion.2), kind=kCustom, calls=%fused_computation | custom fusion | bytes 2099200 | tf_op jit(solution)/shard_map/gather | solution.py:59
  8.0 1.3 broadcast_select_fusion
  9.4 25.3 %all_to_all.20 = bf16[2,32,8,2,512]{4,3,2,0,1:T(2,128)(2,1)S(1)} all-to-all(bf16[2,32,8,2,512]{4,3,2,0,1:T(2,128)(2,1)S(1)} %broadcast_select_fusion), channel_id=1, replica_groups=mesh['fsdp'=32,'grp'=8] {'fsdp'}, dimensions={1} | all-to-all | bytes 2097152 | tf_op jit(solution)/shard_map/all_to_all | solution.py:63
  34.7 0.0 copy-start
  34.7 0.0 copy-start.2
  34.7 2.0 %copy.62 = bf16[2,32,8,2,512]{4,3,1,0,2:T(2,128)(2,1)} copy(bf16[2,32,8,2,512]{4,3,2,0,1:T(2,128)(2,1)S(1)} %all_to_all.20) | data formatting | bytes 2097152 | tf_op jit(solution)/shard_map/all_to_all | solution.py:63
  36.7 8.2 %all-to-all-start.1 = ((bf16[2,32,8,2,512]{4,3,1,0,2:T(2,128)(2,1)}), bf16[2,32,8,2,512]{4,3,1,0,2:T(2,128)(2,1)S(1)}, u32[]{:S(2)}, u32[]{:S(2)}) async-start(bf16[2,32,8,2,512]{4,3,1,0,2:T(2,128)(2,1)} %copy.62), calls=%async_computation.1 | async-start | bytes 2097152 | tf_op jit(solution)/shard_map/all_to_all | solution.py:62
  44.8 1.5 collective-permute-start
  46.3 0.0 copy-done
  46.3 0.0 copy-done.2
  46.3 0.2 fusion.3
  46.5 46.5 %collective-permute-done = bf16[1,2,512,512]{3,2,1,0:T(8,128)(2,1)S(1)} collective-permute-done((bf16[1,2,512,512]{3,2,1,0:T(8,128)(2,1)}, bf16[1,2,512,512]{3,2,1,0:T(8,128)(2,1)S(1)}, u32[]{:S(2)}, u32[]{:S(2)}) %collective-permute-start) | collective-permute-done | bytes 1048608 | tf_op jit(solution)/shard_map/ppermute | solution.py:13
  93.0 3.2 %copy_select_fusion = bf16[2,2,512,512]{3,2,0,1:T(8,128)(2,1)} fusion(bf16[2,2,512,512]{3,2,1,0:T(8,128)(2,1)} %param.12, pred[2]{0:T(512)(128)(4,1)S(1)} %broadcast_compare_fusion, bf16[2,512,512]{2,1,0:T(8,128)(2,1)S(1)} %bitcast.37), kind=kLoop, calls=%fused_computation.3 | loop fusion | flops 1048576 | bytes 5242882 | tf_op jit(solution)/shard_map/jit(_where)/select_n | solution.py:81
  96.2 0.0 all-to-all-done.1
  96.2 1.1 copy.63
  97.4 0.4 reshape.300
  97.8 4.1 %multiply_reduce_fusion = (f32[2]{0:T(128)S(1)}, f32[2,512,512]{2,1,0:T(8,128)}) fusion(bf16[2,2,512,512]{3,2,0,1:T(8,128)(2,1)} %copy_select_fusion, bf16[2,512,512]{2,1,0:T(8,128)(2,1)S(1)} %reshape.300), kind=kOutput, calls=%fused_computation.5 | convolution fusion | flops 1075314688 | bytes 5242888 | tf_op jit(solution)/shard_map/vmap()/dot_general | solution.py:26
  102.0 1.2 multiply_reduce_fusion.1
  103.2 1.9 %multiply_convert_fusion = bf16[2,512,512]{2,1,0:T(8,128)(2,1)S(1)} fusion(f32[2,512,512]{2,1,0:T(8,128)} %get-tuple-element.21, f32[2]{0:T(128)S(1)} %rsqrt_multiply_fusion), kind=kLoop, calls=%fused_computation.4 | loop fusion | flops 1048576 | bytes 3145736 | tf_op jit(solution)/shard_map/vmap()/convert_element_type | solution.py:31
  105.1 0.4 reshape.301
  105.6 1.2 copy.66
  106.7 21.5 %all_to_all.21 = bf16[2,32,8,2,512]{4,3,2,0,1:T(2,128)(2,1)S(1)} all-to-all(bf16[2,32,8,2,512]{4,3,2,0,1:T(2,128)(2,1)S(1)} %copy.66), channel_id=1, replica_groups=mesh['fsdp'=32,'grp'=8] {'fsdp'}, dimensions={1} | all-to-all | bytes 2097152 | tf_op jit(solution)/shard_map/all_to_all | solution.py:88
  128.2 2.0 %copy.67 = bf16[2,32,8,2,512]{4,3,1,0,2:T(2,128)(2,1)} copy(bf16[2,32,8,2,512]{4,3,2,0,1:T(2,128)(2,1)S(1)} %all_to_all.21) | data formatting | bytes 2097152 | tf_op jit(solution)/shard_map/all_to_all | solution.py:88
  130.3 4.3 %all-to-all-start.3 = ((bf16[2,32,8,2,512]{4,3,1,0,2:T(2,128)(2,1)}), bf16[2,32,8,2,512]{4,3,1,0,2:T(2,128)(2,1)S(1)}, u32[]{:S(2)}, u32[]{:S(2)}) async-start(bf16[2,32,8,2,512]{4,3,1,0,2:T(2,128)(2,1)} %copy.67), calls=%async_computation.3 | async-start | bytes 2097152 | tf_op jit(solution)/shard_map/all_to_all | solution.py:87
  134.6 0.1 iota_add_fusion.1
  134.6 0.1 add.244
  134.8 1.9 %gather_fusion.1 = s32[224]{0:T(256)S(1)} fusion(s32[224]{0:T(256)S(1)} %copy-done, s32[1024]{0:T(1024)S(1)} %pad_clamp_fusion.1), kind=kCustom, calls=%fused_computation.1 | custom fusion | bytes 2688 | tf_op jit(solution)/shard_map/gather | solution.py:98
  136.7 0.2 compare_reduce_fusion.1
  136.9 0.0 copy-start.1
  136.9 3.9 %add_select_fusion = f32[2,512,512]{2,1,0:T(8,128)} fusion(f32[2,512,512]{2,1,0:T(8,128)} %param.11, bf16[2,512,512]{2,1,0:T(8,128)(2,1)S(1)} %reshape.300, pred[2]{0:T(512)(128)(4,1)S(1)} %compare_reduce_fusion.1), kind=kOutput, calls=%fused_computation.7 | convolution fusion | flops 538968064 | bytes 5242882 | tf_op jit(solution)/shard_map/vmap()/dot_general | solution.py:20
  140.9 0.0 copy-done.1
  140.9 2.2 %add_select_fusion.1 = f32[2,512,512]{2,1,0:T(8,128)} fusion(f32[2,512,512]{2,1,0:T(8,128)S(1)} %copy-done.1, bf16[2,512,512]{2,1,0:T(8,128)(2,1)S(1)} %reshape.300, pred[2]{0:T(512)(128)(4,1)S(1)} %compare_reduce_fusion.1), kind=kOutput, calls=%fused_computation.8 | convolution fusion | flops 538968064 | bytes 5242882 | tf_op jit(solution)/shard_map/vmap()/dot_general | solution.py:17
  143.1 20.7 %all-to-all-done.3 = bf16[2,32,8,2,512]{4,3,1,0,2:T(2,128)(2,1)S(1)} async-done(((bf16[2,32,8,2,512]{4,3,1,0,2:T(2,128)(2,1)}), bf16[2,32,8,2,512]{4,3,1,0,2:T(2,128)(2,1)S(1)}, u32[]{:S(2)}, u32[]{:S(2)}) %all-to-all-start.3) | async-done | bytes 1048608 | tf_op jit(solution)/shard_map/all_to_all | solution.py:87
  163.8 0.6 copy.68
  164.4 1.1 copy.69
  165.5 2.4 %gather_fusion.2 = bf16[224,2,512]{2,1,0:T(2,128)(2,1)} fusion(bf16[512,2,512]{2,1,0:T(2,128)(2,1)S(1)} %copy.69, s32[1024]{0:T(1024)S(1)} %pad_clamp_fusion), kind=kCustom, calls=%fused_computation.2 | custom fusion | bytes 918400 | tf_op jit(solution)/shard_map/gather | solution.py:100
  (16 shorter events, 0.1 us)
Async XLA Ops:
  34.7 11.6 %copy-start = (s32[224]{0:T(256)S(1)}, s32[224]{0:T(256)}, u32[]{:S(2)}) copy-start(s32[224]{0:T(256)} %param.8) | copy-start | bytes 2692
  34.7 11.6 %copy-start.2 = (s32[224]{0:T(256)S(1)}, s32[224]{0:T(256)}, u32[]{:S(2)}) copy-start(s32[224]{0:T(256)} %param.9) | copy-start | bytes 2692
  36.7 59.6 %all-to-all-start.1 = ((bf16[2,32,8,2,512]{4,3,1,0,2:T(2,128)(2,1)}), bf16[2,32,8,2,512]{4,3,1,0,2:T(2,128)(2,1)S(1)}, u32[]{:S(2)}, u32[]{:S(2)}) async-start(bf16[2,32,8,2,512]{4,3,1,0,2:T(2,128)(2,1)} %copy.62), calls=%async_computation.1 | async-start | bytes 2097152 | tf_op jit(solution)/shard_map/all_to_all | solution.py:62
  44.8 48.2 %collective-permute-start = (bf16[1,2,512,512]{3,2,1,0:T(8,128)(2,1)}, bf16[1,2,512,512]{3,2,1,0:T(8,128)(2,1)S(1)}, u32[]{:S(2)}, u32[]{:S(2)}) collective-permute-start(bf16[1,2,512,512]{3,2,1,0:T(8,128)(2,1)} %param.13), channel_id=1, source_target_pairs={{7,0},{0,1},{1,2},{2,3},{3,4},{4,5},{5,6},{6,7},{15,8},{8,9},{9,10... | collective-permute-start | bytes 3145736 | tf_op jit(solution)/shard_map/ppermute | solution.py:13
  130.3 33.6 %all-to-all-start.3 = ((bf16[2,32,8,2,512]{4,3,1,0,2:T(2,128)(2,1)}), bf16[2,32,8,2,512]{4,3,1,0,2:T(2,128)(2,1)S(1)}, u32[]{:S(2)}, u32[]{:S(2)}) async-start(bf16[2,32,8,2,512]{4,3,1,0,2:T(2,128)(2,1)} %copy.67), calls=%async_computation.3 | async-start | bytes 2097152 | tf_op jit(solution)/shard_map/all_to_all | solution.py:87
  136.9 3.9 %copy-start.1 = (f32[2,512,512]{2,1,0:T(8,128)S(1)}, f32[2,512,512]{2,1,0:T(8,128)}, u32[]{:S(2)}) copy-start(f32[2,512,512]{2,1,0:T(8,128)} %param.10) | copy-start | bytes 6291460
where the time goes:
time: 168 us
  waiting for transfers between devices  67.3 us (40%)
  blocking collectives  46.8 us (28%)
  local copies, waits for them, and re-layouts  18.8 us (11%)
  starting transfers between devices  14 us (8%)
  matrix products  10.3 us (6%)
  other arithmetic  9.93 us (6%)
    ppermute x1, waiting for transfers between devices, shifted(): return lax.ppermute(block, axis, route)  46.5 us
    all_to_all x1, blocking collectives, local(): lax.all_to_all(outbound, 'fsdp', split_axis=1, concat_axis=1, tiled=True)  25.3 us
    all_to_all x1, blocking collectives, local(): lax.all_to_all(outgoing, 'fsdp', split_axis=1, concat_axis=1, tiled=True)  21.5 us
    all_to_all x1, waiting for transfers between devices, local(): lax.all_to_all(lax.all_to_all(outgoing, 'fsdp', split_axis=1, concat_axis...  20.7 us
    all_to_all x1, starting transfers between devices, local(): lax.all_to_all(lax.all_to_all(outbound, 'fsdp', split_axis=1, concat_axis...  8.19 us
    all_to_all x1, starting transfers between devices, local(): lax.all_to_all(lax.all_to_all(outgoing, 'fsdp', split_axis=1, concat_axis...  4.31 us
    dot_general x1, matrix products, slot_work(): jnp.dot(left_applied, inverse_roots[1], preferred_element_type=jnp.float32)  4.13 us
    dot_general x1, matrix products, slot_work(): jnp.dot(piece.T, piece, preferred_element_type=jnp.float32)  3.93 us
  transfers between devices with their start and end apart: 3, of which 2 were waited for; matrix products, arithmetic and copies ran while one was open for 7% of the time, Pallas kernels for 0%

commit v1 on v0

--- a/solution.py
+++ b/solution.py
@@ -1,10 +1,21 @@
+import functools
+
 import jax
 import jax.numpy as jnp
 from jax import lax
+from jax.experimental import pallas as pl
+from jax.experimental.pallas import tpu as pltpu
 from jax.sharding import PartitionSpec as P
 
 decay_rate = 0.999
 epsilon = 1e-06
+
+CHUNKS = 4
+IN_CAP = 56
+OUT_CAP = 48
+ROLES = 3
+
+MESH = pl.DeviceIdType.MESH
 
 
 def shifted(block, axis, distance):
@@ -31,7 +42,7 @@
     return (new_left, new_right, (shaped * graft_scale).astype(jnp.bfloat16))
 
 
-def local(grad, owner, refresh, stats_left, stats_right, old_roots, fresh_roots):
+def dense_plan(grad, owner, refresh, stats_left, stats_right, old_roots, fresh_roots):
     matrices, row_count, width = grad.shape
     capacity, block_size = (stats_left.shape[0], stats_left.shape[1])
     block_cols = width // block_size
@@ -102,6 +113,367 @@
     return (new_left, new_right, update)
 
 
+def make_tables(owner, refresh, fsdp_count, grp_count, capacity, block_cols):
+    my_grp = lax.axis_index("grp")
+    my_device = lax.axis_index("fsdp") * grp_count + my_grp
+    plane_size = fsdp_count * ROLES
+    blocks = jnp.arange(owner.shape[0], dtype=jnp.int32)
+    device, slot = owner // capacity, owner % capacity
+    column, plane = device // grp_count, device % grp_count
+    renewed = refresh == 1
+    root_plane = (plane + grp_count - 1) % grp_count
+    own_role = plane * plane_size + column * ROLES + slot
+    root_role = root_plane * plane_size + column * ROLES + capacity
+    role = jnp.concatenate([own_role, jnp.where(renewed, root_role, -1)])
+    to_plane = jnp.where(role >= 0, role // plane_size, -1)
+    block = jnp.concatenate([blocks, blocks])
+    position = jnp.sum(
+        (to_plane[:, None] == to_plane[None, :]) & (role[:, None] < role[None, :]), axis=0, dtype=jnp.int32
+    )
+    flat = jnp.where(role >= 0, to_plane * IN_CAP + position, -1)
+    block = block % block_cols * (owner.shape[0] // block_cols) + block // block_cols
+    entry = jnp.arange(grp_count * IN_CAP, dtype=jnp.int32)
+    send_block = jnp.sum(jnp.where(flat[None, :] == entry[:, None], block[None, :], 0), axis=1)
+    mine = my_grp * plane_size + jnp.arange(plane_size, dtype=jnp.int32)
+    take = jnp.sum(jnp.where(role[None, :] == mine[:, None], position[None, :], 0), axis=1)
+    out_role = jnp.where(renewed, root_role, own_role)
+    out_plane = out_role // plane_size
+    out_position = jnp.sum(
+        (out_plane[:, None] == out_plane[None, :]) & (out_role[:, None] < out_role[None, :]),
+        axis=0,
+        dtype=jnp.int32,
+    )
+    place = out_plane * OUT_CAP + out_position
+    my_entry = my_grp * OUT_CAP + jnp.arange(OUT_CAP, dtype=jnp.int32)
+    send_role = jnp.sum(
+        jnp.where(place[None, :] == my_entry[:, None], (out_role - out_plane * plane_size)[None, :], 0), axis=1
+    )
+    fits = (jnp.max(jnp.where(role >= 0, position, 0)) < IN_CAP) & (jnp.max(out_position) < OUT_CAP)
+    slots = my_device * capacity + jnp.arange(capacity, dtype=jnp.int32)
+    held = jnp.any(owner[None, :] == slots[:, None], axis=1)
+    keep = jnp.where(held, jnp.float32(decay_rate), jnp.float32(1.0))
+    add = jnp.where(held, jnp.float32(1.0 - decay_rate), jnp.float32(0.0))
+    return fits, send_block, take, send_role, place, jnp.concatenate([keep, add])
+
+
+def step_kernel(
+    sizes,
+    send_block,
+    take,
+    send_role,
+    place,
+    factors,
+    grad_hbm,
+    left_hbm,
+    right_hbm,
+    old_hbm,
+    fresh_hbm,
+    new_left_hbm,
+    new_right_hbm,
+    update,
+    grad,
+    out1,
+    in1,
+    out2,
+    pieces,
+    shaped,
+    in3,
+    out4,
+    in4,
+    roots,
+    left,
+    right,
+    local_sem,
+    self_sem,
+    send_sem,
+    recv_sem,
+):
+    fsdp_count, grp_count, capacity, rows, block, block_cols, matrices = sizes
+    plane_rows = grp_count * rows
+    width = block // CHUNKS
+    f, g = lax.axis_index("fsdp"), lax.axis_index("grp")
+
+    def along(k):
+        return lax.rem(g + k, grp_count)
+
+    def across(k):
+        return lax.rem(f + k, fsdp_count)
+
+    loads = [
+        pltpu.make_async_copy(
+            grad_hbm.at[:, :, pl.ds(j * block, block)],
+            grad.at[pl.ds(j * matrices, matrices)],
+            local_sem.at[0],
+        )
+        for j in range(block_cols)
+    ] + [
+        pltpu.make_async_copy(old_hbm, roots.at[pl.ds(0, capacity)], local_sem.at[1]),
+        pltpu.make_async_copy(fresh_hbm, roots.at[pl.ds(capacity, 1)], local_sem.at[2]),
+        pltpu.make_async_copy(left_hbm, left, local_sem.at[3]),
+        pltpu.make_async_copy(right_hbm, right, local_sem.at[4]),
+    ]
+    for load in loads:
+        load.start()
+
+    barrier = pltpu.get_barrier_semaphore()
+
+    @pl.loop(1, grp_count)
+    def _(k):
+        pl.semaphore_signal(barrier, 1, device_id=(f, along(k)), device_id_type=MESH)
+
+    @pl.loop(1, fsdp_count)
+    def _(k):
+        pl.semaphore_signal(barrier, 1, device_id=(across(k), g), device_id_type=MESH)
+
+    pltpu.make_async_copy(grad, grad, local_sem.at[0]).wait()
+
+    def gather_rows(chunks):
+        @pl.loop(0, grp_count)
+        def _(to):
+            @pl.loop(0, IN_CAP, unroll=8)
+            def _(i):
+                both = grad[send_block[to * IN_CAP + i]]
+                for c in chunks:
+                    out1[c, to, i] = both[:, c * width : (c + 1) * width]
+
+    def grp_copy(c, source, target, k, length, phase):
+        return pltpu.make_async_remote_copy(
+            src_ref=source.at[c, along(k)],
+            dst_ref=target[c].at[pl.ds(g * length, length)],
+            send_sem=send_sem.at[phase, c],
+            recv_sem=recv_sem.at[phase, c],
+            device_id=(f, along(k)),
+            device_id_type=MESH,
+        )
+
+    def grp_wait(c, source, target, length, phase):
+        everything = pltpu.make_async_remote_copy(
+            src_ref=source.at[c, pl.ds(0, grp_count - 1)],
+            dst_ref=target[c].at[pl.ds(0, (grp_count - 1) * length)],
+            send_sem=send_sem.at[phase, c],
+            recv_sem=recv_sem.at[phase, c],
+            device_id=(f, g),
+            device_id_type=MESH,
+        )
+        everything.wait_send()
+        everything.wait_recv()
+
+    def send_rows(c):
+        pltpu.make_async_copy(out1.at[c, g], in1[c].at[pl.ds(g * IN_CAP, IN_CAP)], self_sem.at[0, c]).start()
+
+        @pl.loop(1, grp_count)
+        def _(k):
+            grp_copy(c, out1, in1, k, IN_CAP, 0).start()
+
+    gather_rows([0])
+    pl.semaphore_wait(barrier, grp_count - 1 + fsdp_count - 1)
+    send_rows(0)
+
+    gather_rows(range(1, CHUNKS))
+    for c in range(1, CHUNKS):
+        send_rows(c)
+
+    def spread(c):
+        pltpu.make_async_copy(out1.at[c, g], in1[c].at[pl.ds(g * IN_CAP, IN_CAP)], self_sem.at[0, c]).wait()
+        grp_wait(c, out1, in1, IN_CAP, 0)
+        lanes = pl.ds(c * width, width)
+
+        @pl.loop(0, fsdp_count)
+        def _(k):
+            to = across(k)
+            for role in range(ROLES):
+                i = take[to * ROLES + role]
+                parts = [in1[c][source * IN_CAP + i] for source in range(grp_count)]
+                out2[c, to * ROLES + role] = jnp.concatenate(parts, axis=0)
+
+            source = out2.at[c, pl.ds(to * ROLES, ROLES)]
+            target = pieces.at[:, pl.ds(pl.multiple_of(f * plane_rows, 16), plane_rows), lanes]
+
+            @pl.when(k == 0)
+            def _():
+                pltpu.make_async_copy(source, target, self_sem.at[1, c]).start()
+
+            @pl.when(k > 0)
+            def _():
+                pltpu.make_async_remote_copy(
+                    src_ref=source,
+                    dst_ref=target,
+                    send_sem=send_sem.at[1, c],
+                    recv_sem=recv_sem.at[1, c],
+                    device_id=(to, g),
+                    device_id_type=MESH,
+                ).start()
+
+    for c in range(CHUNKS):
+        spread(c)
+
+    def plane_wait(c, buffer, phase):
+        everything = pltpu.make_async_remote_copy(
+            src_ref=buffer.at[pl.ds(0, (fsdp_count - 1) * ROLES)],
+            dst_ref=buffer.at[pl.ds(0, (fsdp_count - 1) * ROLES)],
+            send_sem=send_sem.at[phase, c],
+            recv_sem=recv_sem.at[phase, c],
+            device_id=(f, g),
+            device_id_type=MESH,
+        )
+        everything.wait_send()
+        everything.wait_recv()
+
+    for c in range(CHUNKS):
+        own = out2.at[c, pl.ds(0, ROLES)]
+        pltpu.make_async_copy(own, own, self_sem.at[1, c]).wait()
+        plane_wait(c, out2.at[c], 1)
+
+    loads[-4].wait()
+    loads[-3].wait()
+
+    @pl.loop(0, ROLES)
+    def _(role):
+        piece = pieces[role]
+        applied = jnp.dot(roots[role, 0], piece, preferred_element_type=jnp.float32).astype(jnp.bfloat16)
+        product = jnp.dot(applied, roots[role, 1], preferred_element_type=jnp.float32)
+        wide = piece.astype(jnp.float32)
+        count = 1.0 / (block * block)
+        scale = jnp.sqrt(jnp.sum(wide * wide, keepdims=True) * count + epsilon) * lax.rsqrt(
+            jnp.sum(product * product, keepdims=True) * count + epsilon
+        )
+        shaped[role] = (product * scale).astype(jnp.bfloat16)
+
+    def send_back(c):
+        lanes = pl.ds(c * width, width)
+
+        @pl.loop(0, fsdp_count)
+        def _(k):
+            to = across(k)
+            source = shaped.at[:, pl.ds(pl.multiple_of(to * plane_rows, 16), plane_rows), lanes]
+            target = in3[c].at[pl.ds(f * ROLES, ROLES)]
+
+            @pl.when(k == 0)
+            def _():
+                pltpu.make_async_copy(source, target, self_sem.at[2, c]).start()
+
+            @pl.when(k > 0)
+            def _():
+                pltpu.make_async_remote_copy(
+                    src_ref=source,
+                    dst_ref=target,
+                    send_sem=send_sem.at[2, c],
+                    recv_sem=recv_sem.at[2, c],
+                    device_id=(to, g),
+                    device_id_type=MESH,
+                ).start()
+
+    for c in range(CHUNKS):
+        send_back(c)
+
+    loads[-2].wait()
+    loads[-1].wait()
+
+    @pl.loop(0, capacity)
+    def _(slot):
+        piece = pieces[slot]
+        keep, add = factors[slot], factors[capacity + slot]
+        outer = lax.dot_general(piece, piece, (((1,), (1,)), ((), ())), preferred_element_type=jnp.float32)
+        left[slot] = keep * left[slot] + add * outer
+        inner = lax.dot_general(piece, piece, (((0,), (0,)), ((), ())), preferred_element_type=jnp.float32)
+        right[slot] = keep * right[slot] + add * inner
+
+    stores = [
+        pltpu.make_async_copy(left, new_left_hbm, local_sem.at[5]),
+        pltpu.make_async_copy(right, new_right_hbm, local_sem.at[6]),
+    ]
+    for store in stores:
+        store.start()
+
+    for c in range(CHUNKS):
+        own = in3[c].at[pl.ds(0, ROLES)]
+        pltpu.make_async_copy(own, own, self_sem.at[2, c]).wait()
+        plane_wait(c, in3[c], 2)
+
+        @pl.loop(0, OUT_CAP, unroll=2)
+        def _(i):
+            tile = in3[c][send_role[i]]
+            for to in range(grp_count):
+                out4[c, to, i] = tile[to * rows : (to + 1) * rows]
+
+        pltpu.make_async_copy(out4.at[c, g], in4[c].at[pl.ds(g * OUT_CAP, OUT_CAP)], self_sem.at[3, c]).start()
+
+        @pl.loop(1, grp_count)
+        def _(k):
+            grp_copy(c, out4, in4, k, OUT_CAP, 3).start()
+
+    for c in range(CHUNKS):
+        pltpu.make_async_copy(out4.at[c, g], in4[c].at[pl.ds(g * OUT_CAP, OUT_CAP)], self_sem.at[3, c]).wait()
+        grp_wait(c, out4, in4, OUT_CAP, 3)
+
+        @pl.loop(0, matrices)
+        def _(m):
+            for j in range(block_cols):
+                column = j * block + c * width
+                update[m, :, pl.ds(column, width)] = in4[c][place[m * block_cols + j]]
+
+    for store in stores:
+        store.wait()
+
+
+def listed_plan(tables, grad, stats_left, stats_right, old_roots, fresh_roots):
+    matrices, rows, total_width = grad.shape
+    capacity, block = stats_left.shape[0], stats_left.shape[1]
+    fsdp_count, grp_count = lax.axis_size("fsdp"), lax.axis_size("grp")
+    sizes = (fsdp_count, grp_count, capacity, rows, block, total_width // block, matrices)
+    width, plane_rows = block // CHUNKS, grp_count * rows
+    bf16 = jnp.bfloat16
+    smem, hbm = pl.BlockSpec(memory_space=pltpu.SMEM), pl.BlockSpec(memory_space=pl.ANY)
+    return pl.pallas_call(
+        functools.partial(step_kernel, sizes),
+        out_shape=(
+            jax.ShapeDtypeStruct(stats_left.shape, jnp.float32),
+            jax.ShapeDtypeStruct(stats_right.shape, jnp.float32),
+            jax.ShapeDtypeStruct(grad.shape, bf16),
+        ),
+        in_specs=[smem] * 5 + [hbm] * 5,
+        out_specs=(hbm, hbm, pl.BlockSpec(memory_space=pltpu.VMEM)),
+        scratch_shapes=[
+            pltpu.VMEM((matrices * (total_width // block), rows, block), bf16),
+            pltpu.VMEM((CHUNKS, grp_count, IN_CAP, rows, width), bf16),
+            [pltpu.VMEM((grp_count * IN_CAP, rows, width), bf16)] * CHUNKS,
+            pltpu.VMEM((CHUNKS, fsdp_count * ROLES, plane_rows, width), bf16),
+            pltpu.VMEM((ROLES, block, block), bf16),
+            pltpu.VMEM((ROLES, block, block), bf16),
+            [pltpu.VMEM((fsdp_count * ROLES, plane_rows, width), bf16)] * CHUNKS,
+            pltpu.VMEM((CHUNKS, grp_count, OUT_CAP, rows, width), bf16),
+            [pltpu.VMEM((grp_count * OUT_CAP, rows, width), bf16)] * CHUNKS,
+            pltpu.VMEM((ROLES, 2, block, block), bf16),
+            pltpu.VMEM(stats_left.shape, jnp.float32),
+            pltpu.VMEM(stats_right.shape, jnp.float32),
+            pltpu.SemaphoreType.DMA((7,)),
+            pltpu.SemaphoreType.DMA((4, CHUNKS)),
+            pltpu.SemaphoreType.DMA((4, CHUNKS)),
+            pltpu.SemaphoreType.DMA((4, CHUNKS)),
+        ],
+        compiler_params=pltpu.CompilerParams(
+            collective_id=1, has_side_effects=True, vmem_limit_bytes=48 * 1024 * 1024
+        ),
+        name="listed_step",
+    )(*tables, grad, stats_left, stats_right, old_roots, fresh_roots)
+
+
+def local(grad, owner, refresh, stats_left, stats_right, old_roots, fresh_roots):
+    fits, *tables = make_tables(
+        owner,
+        refresh,
+        lax.axis_size("fsdp"),
+        lax.axis_size("grp"),
+        stats_left.shape[0],
+        grad.shape[2] // stats_left.shape[1],
+    )
+    return lax.cond(
+        fits,
+        lambda: listed_plan(tables, grad, stats_left, stats_right, old_roots, fresh_roots),
+        lambda: dense_plan(grad, owner, refresh, stats_left, stats_right, old_roots, fresh_roots),
+    )
+
+
 def solution(mesh):
     return jax.shard_map(
         local,

time: 168 us -> 92.4 us (0.55)
  Pallas kernels: 0 us -> 76.7 us
  waiting for transfers between devices: 67.3 us -> 0 us
  blocking collectives: 46.8 us -> 0 us
  starting transfers between devices: 14 us -> 0 us
  local copies, waits for them, and re-layouts: 18.8 us -> 5.42 us
  matrix products: 10.3 us -> 0 us
  other arithmetic: 9.93 us -> 6.71 us
    pallas_call x0 -> x1, Pallas kernels: none -> 76.7 us  [listed_plan(): pl.pallas_call(functools.partial(step_kernel, sizes), out_shape=(jax.Shap...]
    all_to_all x2 -> x0, blocking collectives: 46.8 us -> none  [the longest x1 25.3 us: local(): lax.all_to_all(outbound, 'fsdp', split_axis=1, concat_axis=1, tiled=True)]
    ppermute x1 -> x0, waiting for transfers between devices: 46.5 us -> none  [shifted(): return lax.ppermute(block, axis, route)]
    all_to_all x2 -> x0, waiting for transfers between devices: 20.7 us -> none  [the longest x1 20.7 us: local(): lax.all_to_all(lax.all_to_all(outgoing, 'fsdp', split_axis=1, concat_axis...]
    all_to_all x2 -> x0, starting transfers between devices: 12.5 us -> none  [the longest x1 8.19 us: local(): lax.all_to_all(lax.all_to_all(outbound, 'fsdp', split_axis=1, concat_axis...]
    dot_general x3 -> x0, matrix products: 10.3 us -> none  [the longest x1 4.13 us: slot_work(): jnp.dot(left_applied, inverse_roots[1], preferred_element_type=jnp.float32)]
    gather x3 -> x0, local copies, waits for them, and re-layouts: 7.87 us -> none  [the longest x1 3.56 us: local(): local_blocks[local_index]]
    all_to_all x4 -> x0, local copies, waits for them, and re-layouts: 5.71 us -> none  [the longest x1 2 us: local(): lax.all_to_all(outgoing, 'fsdp', split_axis=1, concat_axis=1, tiled=True)]
  transfers between devices with their start and end apart: 3 -> 0, of which waited for: 2 -> 0; matrix products, arithmetic and copies ran while one was open for 7% -> 0% of each run, Pallas kernels for 0% -> 0%
where the time goes in v1:
time: 92.4 us; the launch traced here: 90.8 us
  Pallas kernels  76.7 us (83%)
  other arithmetic  6.71 us (7%)
  local copies, waits for them, and re-layouts  5.42 us (6%)
  between operations  2 us (2%)
    pallas_call x1, Pallas kernels, listed_plan(): pl.pallas_call(functools.partial(step_kernel, sizes), out_shape=(jax.Shap...  76.7 us
    unnamed x7, local copies, waits for them, and re-layouts  4.43 us

profile of v1, /device:TPU:1, one launch (start us, length us, event | category | flops | bytes accessed | tf_op | source)
XLA Modules:
  0.0 90.8 jit_solution(10232621163022101548)
XLA Ops:
  0.6 0.9 compare_reduce_fusion.2
  1.5 0.1 pad_maximum_fusion
  1.6 0.7 fusion.15
  2.3 0.7 and_select_fusion.7
  3.0 0.7 broadcast_select_fusion.1
  3.7 0.1 convert_reduce_fusion.1
  3.9 0.6 reduce_max.19
  5.2 0.1 pad_add_fusion.1
  5.2 0.1 fusion.8
  5.3 0.2 convert_reduce_fusion
  5.6 0.7 select_reduce_fusion.3
  6.9 1.0 %eq.162 = s32[448,448]{1,0:T(8,128)} iota(), iota_dimension=0 | iota | bytes 802816 | tf_op jit(solution)/shard_map/eq | solution.py:136
  7.9 78.5 %conditional.1 = ((f32[2,512,512]{2,1,0:T(8,128)S(1)}, f32[2,512,512]{2,1,0:T(8,128)}, bf16[16,2,7168]{2,1,0:T(2,128)(2,1)})) conditional(s32[]{:T(128)} %convert_element_type.28, (s32[224]{0:T(256)}, f32[2,512,512]{2,1,0:T(8,128)}, bf16[16,2,7168]{2,1,0:T(2,128)(2,1)}, f32[2,512,512]{2,1,0:T(8,128)}, s32[224]{0:T(256)}, ...), branch_computations={%region_5.12_spmd, %region_12.16_spmd} | conditional | flops 2158039552 | bytes 84615936 | solution.py:470
  7.9 0.2 select_reduce_fusion.1.take
  8.2 1.4 %select_reduce_fusion.send_block = s32[448]{0:T(512)S(1)} fusion(s32[448,448]{1,0:T(8,128)} %get-tuple-element.174, s32[448]{0:T(512)S(1)} %bitcast.52, s32[448]{0:T(512)S(1)} %bitcast.51), kind=kLoop, calls=%fused_computation.3 | loop fusion | flops 601664 | bytes 808192 | tf_op jit(solution)/shard_map/reduce_sum | solution.py:136
  9.5 0.2 select_reduce_fusion.2.send_role
  9.7 76.7 %listed_step.1 = (f32[2,512,512]{2,1,0:T(8,128)S(1)}, f32[2,512,512]{2,1,0:T(8,128)}, bf16[16,2,7168]{2,1,0:T(2,128)(2,1)}) custom-call(s32[448]{0:T(512)S(1)} %select_reduce_fusion.send_block, s32[96]{0:T(128)S(1)} %select_reduce_fusion.1.take, s32[48]{0:T(128)S(1)} %select_reduce_fusion.2.send_role, s32[224]{0:T(256)S(1)} %get-tuple-element.291.place, ...), custom_call_target="tpu_custom_call" | custom-call | tf_op jit(solution)/shard_map/cond/branch_1_fun/listed_step/pallas_call | solution.py:427
  86.4 0.0 copy-start.3
  86.4 1.3 %copy.106 = f32[2,512,512]{2,1,0:T(8,128)} copy(f32[2,512,512]{2,1,0:T(8,128)S(1)} %get-tuple-element.314) | data formatting | bytes 4194304
  87.7 1.0 %copy-done.3 = f32[2,512,512]{2,1,0:T(8,128)S(1)} copy-done((f32[2,512,512]{2,1,0:T(8,128)S(1)}, f32[2,512,512]{2,1,0:T(8,128)}, u32[]{:S(2)}) %copy-start.3) | copy-done | bytes 2097176
  88.7 0.0 copy-start.4
  88.7 1.3 %copy.107 = f32[2,512,512]{2,1,0:T(8,128)} copy(f32[2,512,512]{2,1,0:T(8,128)S(1)} %copy-done.3) | data formatting | bytes 4194304
  90.1 0.0 copy-done.4
  90.1 0.8 copy.108
  (10 shorter events, 0.1 us)
Async XLA Ops:
  86.4 2.3 %copy-start.3 = (f32[2,512,512]{2,1,0:T(8,128)S(1)}, f32[2,512,512]{2,1,0:T(8,128)}, u32[]{:S(2)}) copy-start(f32[2,512,512]{2,1,0:T(8,128)} %get-tuple-element.315) | copy-start | bytes 6291460
  88.7 1.3 %copy-start.4 = (bf16[16,2,7168]{2,1,0:T(2,128)(2,1)S(1)}, bf16[16,2,7168]{2,1,0:T(2,128)(2,1)}, u32[]{:S(2)}) copy-start(bf16[16,2,7168]{2,1,0:T(2,128)(2,1)} %get-tuple-element.316) | copy-start | bytes 1376260

commit v2 on v1

--- a/solution.py
+++ b/solution.py
@@ -11,8 +11,8 @@
 epsilon = 1e-06
 
 CHUNKS = 4
-IN_CAP = 56
-OUT_CAP = 48
+IN_CAP = 52
+OUT_CAP = 42
 ROLES = 3
 
 MESH = pl.DeviceIdType.MESH
@@ -113,9 +113,7 @@
     return (new_left, new_right, update)
 
 
-def make_tables(owner, refresh, fsdp_count, grp_count, capacity, block_cols):
-    my_grp = lax.axis_index("grp")
-    my_device = lax.axis_index("fsdp") * grp_count + my_grp
+def make_roles(owner, refresh, fsdp_count, grp_count, capacity, block_cols):
     plane_size = fsdp_count * ROLES
     blocks = jnp.arange(owner.shape[0], dtype=jnp.int32)
     device, slot = owner // capacity, owner % capacity
@@ -124,45 +122,71 @@
     root_plane = (plane + grp_count - 1) % grp_count
     own_role = plane * plane_size + column * ROLES + slot
     root_role = root_plane * plane_size + column * ROLES + capacity
-    role = jnp.concatenate([own_role, jnp.where(renewed, root_role, -1)])
-    to_plane = jnp.where(role >= 0, role // plane_size, -1)
-    block = jnp.concatenate([blocks, blocks])
-    position = jnp.sum(
-        (to_plane[:, None] == to_plane[None, :]) & (role[:, None] < role[None, :]), axis=0, dtype=jnp.int32
-    )
-    flat = jnp.where(role >= 0, to_plane * IN_CAP + position, -1)
-    block = block % block_cols * (owner.shape[0] // block_cols) + block // block_cols
-    entry = jnp.arange(grp_count * IN_CAP, dtype=jnp.int32)
-    send_block = jnp.sum(jnp.where(flat[None, :] == entry[:, None], block[None, :], 0), axis=1)
-    mine = my_grp * plane_size + jnp.arange(plane_size, dtype=jnp.int32)
-    take = jnp.sum(jnp.where(role[None, :] == mine[:, None], position[None, :], 0), axis=1)
-    out_role = jnp.where(renewed, root_role, own_role)
-    out_plane = out_role // plane_size
-    out_position = jnp.sum(
-        (out_plane[:, None] == out_plane[None, :]) & (out_role[:, None] < out_role[None, :]),
-        axis=0,
-        dtype=jnp.int32,
-    )
-    place = out_plane * OUT_CAP + out_position
-    my_entry = my_grp * OUT_CAP + jnp.arange(OUT_CAP, dtype=jnp.int32)
-    send_role = jnp.sum(
-        jnp.where(place[None, :] == my_entry[:, None], (out_role - out_plane * plane_size)[None, :], 0), axis=1
-    )
-    fits = (jnp.max(jnp.where(role >= 0, position, 0)) < IN_CAP) & (jnp.max(out_position) < OUT_CAP)
-    slots = my_device * capacity + jnp.arange(capacity, dtype=jnp.int32)
-    held = jnp.any(owner[None, :] == slots[:, None], axis=1)
-    keep = jnp.where(held, jnp.float32(decay_rate), jnp.float32(1.0))
-    add = jnp.where(held, jnp.float32(1.0 - decay_rate), jnp.float32(0.0))
-    return fits, send_block, take, send_role, place, jnp.concatenate([keep, add])
+    out_plane = jnp.where(renewed, root_plane, plane)
+    order = blocks % block_cols * (owner.shape[0] // block_cols) + blocks // block_cols
+    rows = (
+        own_role,
+        jnp.where(renewed, root_role, -1),
+        jnp.where(renewed, root_role, own_role),
+        plane * plane_size,
+        root_plane * plane_size,
+        out_plane * plane_size,
+        plane * IN_CAP,
+        root_plane * IN_CAP,
+        out_plane * OUT_CAP,
+        order,
+    )
+    roles = jnp.stack(rows)
+    planes = jnp.arange(grp_count, dtype=jnp.int32)[:, None]
+    owned = (plane[None, :] == planes).astype(jnp.int32)
+    moved = ((root_plane[None, :] == planes) & renewed[None, :]).astype(jnp.int32)
+    left_over = ((plane[None, :] == planes) & ~renewed[None, :]).astype(jnp.int32)
+    over = jnp.maximum(jnp.sum(owned + moved, axis=1) - IN_CAP, jnp.sum(left_over + moved, axis=1) - OUT_CAP)
+    return jnp.max(over) <= 0, roles
+
+
+def fill_table(roles, table, my_grp, grp_count, plane_size):
+    count = roles.shape[1]
+    i32 = jnp.int32
+
+    def spot(shape, axis):
+        return lax.broadcasted_iota(i32, shape, axis)
+
+    diagonal = spot((count, count), 0) == spot((count, count), 1)
+
+    def upright(row):
+        return jnp.sum(jnp.where(diagonal, roles[row : row + 1], 0), axis=1, keepdims=True)
+
+    own, root, out, own_start, root_start, out_start, own_base, root_base, out_base, order = map(
+        upright, range(10)
+    )
+    own_row, root_row, out_row = roles[0:1], roles[1:2], roles[2:3]
+
+    def ahead(row, start, role):
+        return jnp.sum(((row >= start) & (row < role)).astype(i32), axis=1, keepdims=True)
+
+    own_at = ahead(own_row, own_start, own) + ahead(root_row, own_start, own)
+    root_at = ahead(own_row, root_start, root) + ahead(root_row, root_start, root)
+    out_at = ahead(out_row, out_start, out)
+
+    def pick(key, wanted, value):
+        return jnp.sum(jnp.where(key == wanted, value, 0), axis=0, keepdims=True)
+
+    length = grp_count * IN_CAP
+    entry = spot((count, length), 1)
+    root_entry = jnp.where(root >= 0, root_base + root_at, -1)
+    table[0:1, 0:length] = pick(own_base + own_at, entry, order) + pick(root_entry, entry, order)
+    mine = my_grp * plane_size + spot((count, plane_size), 1)
+    table[1:2, 0:plane_size] = pick(own, mine, own_at) + pick(root, mine, root_at)
+    place = out_base + out_at
+    table[2:3, 0:count] = jnp.sum(jnp.where(diagonal, place, 0), axis=0, keepdims=True)
+    my_entry = my_grp * OUT_CAP + spot((count, OUT_CAP), 1)
+    table[3:4, 0:OUT_CAP] = pick(place, my_entry, out - out_start)
 
 
 def step_kernel(
     sizes,
-    send_block,
-    take,
-    send_role,
-    place,
-    factors,
+    roles,
     grad_hbm,
     left_hbm,
     right_hbm,
@@ -176,6 +200,7 @@
     in1,
     out2,
     pieces,
+    product,
     shaped,
     in3,
     out4,
@@ -183,6 +208,8 @@
     roots,
     left,
     right,
+    table,
+    lookup,
     local_sem,
     self_sem,
     send_sem,
@@ -225,14 +252,18 @@
     def _(k):
         pl.semaphore_signal(barrier, 1, device_id=(across(k), g), device_id_type=MESH)
 
+    fill_table(roles, table, g, grp_count, fsdp_count * ROLES)
+    to_scalars = pltpu.make_async_copy(table, lookup, local_sem.at[5])
+    to_scalars.start()
     pltpu.make_async_copy(grad, grad, local_sem.at[0]).wait()
+    to_scalars.wait()
 
     def gather_rows(chunks):
         @pl.loop(0, grp_count)
         def _(to):
             @pl.loop(0, IN_CAP, unroll=8)
             def _(i):
-                both = grad[send_block[to * IN_CAP + i]]
+                both = grad[lookup[0, to * IN_CAP + i]]
                 for c in chunks:
                     out1[c, to, i] = both[:, c * width : (c + 1) * width]
 
@@ -282,7 +313,7 @@
         def _(k):
             to = across(k)
             for role in range(ROLES):
-                i = take[to * ROLES + role]
+                i = lookup[1, to * ROLES + role]
                 parts = [in1[c][source * IN_CAP + i] for source in range(grp_count)]
                 out2[c, to * ROLES + role] = jnp.concatenate(parts, axis=0)
 
@@ -319,25 +350,34 @@
         everything.wait_send()
         everything.wait_recv()
 
+    def apply_left(h):
+        lanes = pl.ds(h * (block // 2), block // 2)
+
+        @pl.loop(0, ROLES)
+        def _(role):
+            piece = pieces[role, :, lanes]
+            applied = jnp.dot(roots[role, 0], piece, preferred_element_type=jnp.float32).astype(jnp.bfloat16)
+            share = jnp.dot(applied, roots[role, 1, lanes, :], preferred_element_type=jnp.float32)
+            if h == 0:
+                product[role] = share
+            else:
+                total = product[role] + share
+                wide = pieces[role].astype(jnp.float32)
+                count = 1.0 / (block * block)
+                scale = jnp.sqrt(jnp.sum(wide * wide, keepdims=True) * count + epsilon) * lax.rsqrt(
+                    jnp.sum(total * total, keepdims=True) * count + epsilon
+                )
+                shaped[role] = (total * scale).astype(jnp.bfloat16)
+
+    loads[-4].wait()
+    loads[-3].wait()
     for c in range(CHUNKS):
         own = out2.at[c, pl.ds(0, ROLES)]
         pltpu.make_async_copy(own, own, self_sem.at[1, c]).wait()
         plane_wait(c, out2.at[c], 1)
-
-    loads[-4].wait()
-    loads[-3].wait()
-
-    @pl.loop(0, ROLES)
-    def _(role):
-        piece = pieces[role]
-        applied = jnp.dot(roots[role, 0], piece, preferred_element_type=jnp.float32).astype(jnp.bfloat16)
-        product = jnp.dot(applied, roots[role, 1], preferred_element_type=jnp.float32)
-        wide = piece.astype(jnp.float32)
-        count = 1.0 / (block * block)
-        scale = jnp.sqrt(jnp.sum(wide * wide, keepdims=True) * count + epsilon) * lax.rsqrt(
-            jnp.sum(product * product, keepdims=True) * count + epsilon
-        )
-        shaped[role] = (product * scale).astype(jnp.bfloat16)
+        if c == CHUNKS // 2 - 1:
+            apply_left(0)
+    apply_left(1)
 
     def send_back(c):
         lanes = pl.ds(c * width, width)
@@ -363,45 +403,50 @@
                     device_id_type=MESH,
                 ).start()
 
-    for c in range(CHUNKS):
-        send_back(c)
-
-    loads[-2].wait()
-    loads[-1].wait()
-
-    @pl.loop(0, capacity)
-    def _(slot):
+    def return_rows(c):
+        own = in3[c].at[pl.ds(0, ROLES)]
+        pltpu.make_async_copy(own, own, self_sem.at[2, c]).wait()
+        plane_wait(c, in3[c], 2)
+
+        @pl.loop(0, OUT_CAP, unroll=2)
+        def _(i):
+            tile = in3[c][lookup[3, i]]
+            for to in range(grp_count):
+                out4[c, to, i] = tile[to * rows : (to + 1) * rows]
+
+        pltpu.make_async_copy(out4.at[c, g], in4[c].at[pl.ds(g * OUT_CAP, OUT_CAP)], self_sem.at[3, c]).start()
+
+        @pl.loop(1, grp_count)
+        def _(k):
+            grp_copy(c, out4, in4, k, OUT_CAP, 3).start()
+
+    def update_statistics(slot):
         piece = pieces[slot]
-        keep, add = factors[slot], factors[capacity + slot]
+        held = jnp.sum((roles[0:1] == (g * fsdp_count + f) * ROLES + slot).astype(jnp.int32), axis=1, keepdims=True) > 0
+        keep = jnp.where(held, jnp.float32(decay_rate), jnp.float32(1.0))
+        add = jnp.where(held, jnp.float32(1.0 - decay_rate), jnp.float32(0.0))
         outer = lax.dot_general(piece, piece, (((1,), (1,)), ((), ())), preferred_element_type=jnp.float32)
         left[slot] = keep * left[slot] + add * outer
         inner = lax.dot_general(piece, piece, (((0,), (0,)), ((), ())), preferred_element_type=jnp.float32)
         right[slot] = keep * right[slot] + add * inner
 
+    send_back(0)
+    send_back(1)
+    for c in range(2, CHUNKS):
+        return_rows(c - 2)
+        send_back(c)
+    loads[-2].wait()
+    loads[-1].wait()
+    pl.loop(0, 1)(update_statistics)
+    return_rows(CHUNKS - 2)
+    return_rows(CHUNKS - 1)
+    pl.loop(1, capacity)(update_statistics)
     stores = [
         pltpu.make_async_copy(left, new_left_hbm, local_sem.at[5]),
         pltpu.make_async_copy(right, new_right_hbm, local_sem.at[6]),
     ]
     for store in stores:
         store.start()
-
-    for c in range(CHUNKS):
-        own = in3[c].at[pl.ds(0, ROLES)]
-        pltpu.make_async_copy(own, own, self_sem.at[2, c]).wait()
-        plane_wait(c, in3[c], 2)
-
-        @pl.loop(0, OUT_CAP, unroll=2)
-        def _(i):
-            tile = in3[c][send_role[i]]
-            for to in range(grp_count):
-                out4[c, to, i] = tile[to * rows : (to + 1) * rows]
-
-        pltpu.make_async_copy(out4.at[c, g], in4[c].at[pl.ds(g * OUT_CAP, OUT_CAP)], self_sem.at[3, c]).start()
-
-        @pl.loop(1, grp_count)
-        def _(k):
-            grp_copy(c, out4, in4, k, OUT_CAP, 3).start()
-
     for c in range(CHUNKS):
         pltpu.make_async_copy(out4.at[c, g], in4[c].at[pl.ds(g * OUT_CAP, OUT_CAP)], self_sem.at[3, c]).wait()
         grp_wait(c, out4, in4, OUT_CAP, 3)
@@ -410,20 +455,20 @@
         def _(m):
             for j in range(block_cols):
                 column = j * block + c * width
-                update[m, :, pl.ds(column, width)] = in4[c][place[m * block_cols + j]]
+                update[m, :, pl.ds(column, width)] = in4[c][lookup[2, m * block_cols + j]]
 
     for store in stores:
         store.wait()
 
 
-def listed_plan(tables, grad, stats_left, stats_right, old_roots, fresh_roots):
+def listed_plan(roles, grad, stats_left, stats_right, old_roots, fresh_roots):
     matrices, rows, total_width = grad.shape
     capacity, block = stats_left.shape[0], stats_left.shape[1]
     fsdp_count, grp_count = lax.axis_size("fsdp"), lax.axis_size("grp")
     sizes = (fsdp_count, grp_count, capacity, rows, block, total_width // block, matrices)
     width, plane_rows = block // CHUNKS, grp_count * rows
     bf16 = jnp.bfloat16
-    smem, hbm = pl.BlockSpec(memory_space=pltpu.SMEM), pl.BlockSpec(memory_space=pl.ANY)
+    vmem, hbm = pl.BlockSpec(memory_space=pltpu.VMEM), pl.BlockSpec(memory_space=pl.ANY)
     return pl.pallas_call(
         functools.partial(step_kernel, sizes),
         out_shape=(
@@ -431,14 +476,15 @@
             jax.ShapeDtypeStruct(stats_right.shape, jnp.float32),
             jax.ShapeDtypeStruct(grad.shape, bf16),
         ),
-        in_specs=[smem] * 5 + [hbm] * 5,
-        out_specs=(hbm, hbm, pl.BlockSpec(memory_space=pltpu.VMEM)),
+        in_specs=[vmem] + [hbm] * 5,
+        out_specs=(hbm, hbm, vmem),
         scratch_shapes=[
             pltpu.VMEM((matrices * (total_width // block), rows, block), bf16),
             pltpu.VMEM((CHUNKS, grp_count, IN_CAP, rows, width), bf16),
             [pltpu.VMEM((grp_count * IN_CAP, rows, width), bf16)] * CHUNKS,
             pltpu.VMEM((CHUNKS, fsdp_count * ROLES, plane_rows, width), bf16),
             pltpu.VMEM((ROLES, block, block), bf16),
+            pltpu.VMEM((ROLES, block, block), jnp.float32),
             pltpu.VMEM((ROLES, block, block), bf16),
             [pltpu.VMEM((fsdp_count * ROLES, plane_rows, width), bf16)] * CHUNKS,
             pltpu.VMEM((CHUNKS, grp_count, OUT_CAP, rows, width), bf16),
@@ -446,20 +492,22 @@
             pltpu.VMEM((ROLES, 2, block, block), bf16),
             pltpu.VMEM(stats_left.shape, jnp.float32),
             pltpu.VMEM(stats_right.shape, jnp.float32),
+            pltpu.VMEM((8, 512), jnp.int32),
+            pltpu.SMEM((8, 512), jnp.int32),
             pltpu.SemaphoreType.DMA((7,)),
             pltpu.SemaphoreType.DMA((4, CHUNKS)),
             pltpu.SemaphoreType.DMA((4, CHUNKS)),
             pltpu.SemaphoreType.DMA((4, CHUNKS)),
         ],
         compiler_params=pltpu.CompilerParams(
-            collective_id=1, has_side_effects=True, vmem_limit_bytes=48 * 1024 * 1024
+            collective_id=1, has_side_effects=True, vmem_limit_bytes=28 * 1024 * 1024
         ),
         name="listed_step",
-    )(*tables, grad, stats_left, stats_right, old_roots, fresh_roots)
+    )(roles, grad, stats_left, stats_right, old_roots, fresh_roots)
 
 
 def local(grad, owner, refresh, stats_left, stats_right, old_roots, fresh_roots):
-    fits, *tables = make_tables(
+    fits, roles = make_roles(
         owner,
         refresh,
         lax.axis_size("fsdp"),
@@ -469,7 +517,7 @@
     )
     return lax.cond(
         fits,
-        lambda: listed_plan(tables, grad, stats_left, stats_right, old_roots, fresh_roots),
+        lambda: listed_plan(roles, grad, stats_left, stats_right, old_roots, fresh_roots),
         lambda: dense_plan(grad, owner, refresh, stats_left, stats_right, old_roots, fresh_roots),
     )
 

time: 92.4 us -> 82.4 us (0.89); the launches traced: 90.8 us -> 82.2 us
  other arithmetic: 6.71 us -> 2.24 us
  Pallas kernels: 76.7 us -> 73.2 us
    pallas_call x1, Pallas kernels: 76.7 us -> 73.2 us  [listed_plan(): pl.pallas_call(functools.partial(step_kernel, sizes), out_shape=(jax.Shap...]
    reduce_sum x5 -> x1, other arithmetic: 2.09 us -> 0.15 us  [make_roles(): jnp.sum(owned + moved, axis=1) - IN_CAP]
    select_n x5 -> x0, other arithmetic: 1.54 us -> none  [the longest x1 0.73 us: make_tables(): out_plane = out_role // plane_size]
    eq x1 -> x0, local copies, waits for them, and re-layouts: 0.98 us -> none  [make_tables(): flat[None, :] == entry[:, None]]
    unnamed x7 -> x5, local copies, waits for them, and re-layouts: 4.43 us -> 5.17 us
where the time goes in v2:
time: 82.4 us; the launch traced here: 82.2 us
  Pallas kernels  73.2 us (89%)
  local copies, waits for them, and re-layouts  5.22 us (6%)
  other arithmetic  2.24 us (3%)
  between operations  1.31 us (2%)
    pallas_call x1, Pallas kernels, listed_plan(): pl.pallas_call(functools.partial(step_kernel, sizes), out_shape=(jax.Shap...  73.2 us
    unnamed x5, local copies, waits for them, and re-layouts  5.17 us

profile of v2, /device:TPU:1, one launch (start us, length us, event | category | flops | bytes accessed | tf_op | source)
XLA Modules:
  0.0 82.2 jit_solution(16909750031785823906)
XLA Ops:
  0.7 0.7 broadcast_multiply_fusion
  1.4 0.1 fusion.6
  1.5 0.6 maximum_reduce_fusion
  2.8 0.7 broadcast_multiply_fusion.2
  3.5 0.1 stack.40
  3.6 73.4 %conditional.1 = ((f32[2,512,512]{2,1,0:T(8,128)}, f32[2,512,512]{2,1,0:T(8,128)S(1)}, bf16[16,2,7168]{2,1,0:T(2,128)(2,1)})) conditional(s32[]{:T(128)} %convert_element_type.32, (s32[224]{0:T(256)}, f32[2,512,512]{2,1,0:T(8,128)}, bf16[16,2,7168]{2,1,0:T(2,128)(2,1)}, f32[2,512,512]{2,1,0:T(8,128)}, s32[224]{0:T(256)}, ...), branch_computations={%region_3.10_spmd, %region_10.11_spmd} | conditional | flops 2158039552 | bytes 76227296 | solution.py:518
  3.8 73.2 %listed_step.1 = (f32[2,512,512]{2,1,0:T(8,128)}, f32[2,512,512]{2,1,0:T(8,128)S(1)}, bf16[16,2,7168]{2,1,0:T(2,128)(2,1)}) custom-call(s32[10,224]{1,0:T(8,128)S(1)} %get-tuple-element.33.roles, bf16[16,2,7168]{2,1,0:T(2,128)(2,1)} %get-tuple-element.34.grad_hbm, f32[2,512,512]{2,1,0:T(8,128)} %get-tuple-element.35.left_hbm, ...), custom_call_target="tpu_custom_call" | custom-call | tf_op jit(solution)/shard_map/cond/branch_1_fun/listed_step/pallas_call | solution.py:472
  77.1 3.1 %copy.106 = f32[2,512,512]{2,1,0:T(8,128)} copy(f32[2,512,512]{2,1,0:T(8,128)} %get-tuple-element.168) | data formatting | bytes 4194304
  80.1 0.0 copy-start.2
  80.1 1.3 %copy.107 = f32[2,512,512]{2,1,0:T(8,128)} copy(f32[2,512,512]{2,1,0:T(8,128)S(1)} %get-tuple-element.169) | data formatting | bytes 4194304
  81.5 0.0 copy-done.2
  81.5 0.8 copy.108
  (3 shorter events, 0.0 us)
Async XLA Ops:
  80.1 1.3 %copy-start.2 = (bf16[16,2,7168]{2,1,0:T(2,128)(2,1)S(1)}, bf16[16,2,7168]{2,1,0:T(2,128)(2,1)}, u32[]{:S(2)}) copy-start(bf16[16,2,7168]{2,1,0:T(2,128)(2,1)} %get-tuple-element.170) | copy-start | bytes 1376260

commit v3 on v0

--- a/solution.py
+++ b/solution.py
@@ -1,10 +1,20 @@
+import functools
+
 import jax
 import jax.numpy as jnp
+import numpy as np
 from jax import lax
+from jax.experimental import pallas as pl
+from jax.experimental.pallas import tpu as pltpu
 from jax.sharding import PartitionSpec as P
 
 decay_rate = 0.999
 epsilon = 1e-06
+
+CHUNKS = 4
+LISTS = ((48, 38), (64, 56))
+
+MESH = pl.DeviceIdType.MESH
 
 
 def shifted(block, axis, distance):
@@ -31,7 +41,7 @@
     return (new_left, new_right, (shaped * graft_scale).astype(jnp.bfloat16))
 
 
-def local(grad, owner, refresh, stats_left, stats_right, old_roots, fresh_roots):
+def dense_plan(grad, owner, refresh, stats_left, stats_right, old_roots, fresh_roots):
     matrices, row_count, width = grad.shape
     capacity, block_size = (stats_left.shape[0], stats_left.shape[1])
     block_cols = width // block_size
@@ -102,6 +112,436 @@
     return (new_left, new_right, update)
 
 
+def halves(value, size):
+    if size & (size - 1):
+        return value // size, value % size
+    return value >> (size.bit_length() - 1), value & (size - 1)
+
+
+def too_short(owner, refresh, grp_count, capacity):
+    plane = halves(halves(owner, capacity)[0], grp_count)[1]
+    planes = np.arange(grp_count, dtype=np.int32)
+    here = plane[None, :] == planes[:, None]
+    there = plane[None, :] == np.roll(planes, -1)[:, None]
+    owned = here.astype(jnp.int32)
+    due = jnp.sum(owned + jnp.where(there, refresh[None, :], 0), axis=1)
+    kept = jnp.sum(owned, axis=1)
+    over = [jnp.max(jnp.maximum(due - here, kept - back)) > 0 for here, back in LISTS]
+    return sum(each.astype(jnp.int32) for each in over)
+
+
+def fill_table(owner_row, refresh_row, table, my_grp, fsdp_count, grp_count, capacity, block_cols, lengths):
+    count, roles = owner_row.shape[1], capacity + 1
+    in_length, out_length = lengths
+    i32 = jnp.int32
+
+    def spot(shape, axis):
+        return lax.broadcasted_iota(i32, shape, axis)
+
+    diagonal = spot((count, count), 0) == spot((count, count), 1)
+
+    def upright(row):
+        return jnp.sum(jnp.where(diagonal, row, 0), axis=1, keepdims=True)
+
+    def views(owner, renewed):
+        device, slot = halves(owner, capacity)
+        column, plane = halves(device, grp_count)
+        root_plane = jnp.where(plane == 0, grp_count - 1, plane - 1)
+        own = (plane * fsdp_count + column) * roles + slot
+        root = jnp.where(renewed, (root_plane * fsdp_count + column) * roles + capacity, -1)
+        return plane, root_plane, column * capacity + slot, own, root
+
+    _, _, _, own_row, root_row = views(owner_row, refresh_row == 1)
+    renewed = upright(refresh_row) == 1
+    plane, root_plane, home, own, root = views(upright(owner_row), renewed)
+    own_start, root_start = plane * (fsdp_count * roles), root_plane * (fsdp_count * roles)
+
+    def ahead(row, start, role):
+        return jnp.sum(((row >= start) & (row < role)).astype(i32), axis=1, keepdims=True)
+
+    out_at = ahead(own_row, own_start, own)
+    own_at = out_at + ahead(root_row, own_start, own)
+    root_at = ahead(own_row, root_start, root) + ahead(root_row, root_start, root)
+
+    def pick(key, base, length, value):
+        wanted = base + spot((count, length), 1)
+        return jnp.sum(jnp.where(key == wanted, value, 0), axis=0, keepdims=True)
+
+    block = spot((count, 1), 0)
+    matrix = sum((block >= block_cols * m).astype(i32) for m in range(1, count // block_cols))
+    order = (block - matrix * block_cols) * (count // block_cols) + matrix
+    root_entry = jnp.where(renewed, root_plane * in_length + root_at, -1)
+    length, plane_size = grp_count * in_length, fsdp_count * roles
+
+    def put(row, values, limit):
+        table[row : row + 1, 0 : values.shape[1]] = jnp.clip(values, 0, limit - 1)
+
+    put(0, pick(plane * in_length + own_at, 0, length, order) + pick(root_entry, 0, length, order), count)
+    put(1, pick(own, my_grp * plane_size, plane_size, own_at) + pick(root, my_grp * plane_size, plane_size, root_at), in_length)
+    place = plane * out_length + out_at
+    put(2, jnp.sum(jnp.where(diagonal, place, 0), axis=0, keepdims=True), grp_count * out_length)
+    put(3, pick(place, my_grp * out_length, out_length, home), fsdp_count * capacity)
+
+
+def both_ways(count):
+    return [k for near in range(count // 2, 0, -1) for k in dict.fromkeys((near, count - near))]
+
+
+def step_kernel(
+    sizes,
+    lengths,
+    owner_row,
+    refresh_row,
+    grad_hbm,
+    left_hbm,
+    right_hbm,
+    old_hbm,
+    fresh_hbm,
+    new_left_hbm,
+    new_right_hbm,
+    update,
+    grad,
+    out1,
+    in1,
+    out2,
+    pieces,
+    product,
+    shaped,
+    back,
+    settled,
+    in3,
+    out4,
+    in4,
+    roots,
+    left,
+    right,
+    table,
+    lookup,
+    local_sem,
+    self_sem,
+    send_sem,
+    recv_sem,
+):
+    fsdp_count, grp_count, capacity, rows, block, block_cols, matrices = sizes
+    plane_rows = grp_count * rows
+    width = block // CHUNKS
+    f, g = lax.axis_index("fsdp"), lax.axis_index("grp")
+    roles_in = capacity + 1
+    in_length, out_length = lengths
+
+    def along(k):
+        return lax.rem(g + k, grp_count)
+
+    def across(k):
+        return lax.rem(f + k, fsdp_count)
+
+    loads = [
+        pltpu.make_async_copy(
+            grad_hbm.at[:, :, pl.ds(j * block, block)],
+            grad.at[pl.ds(j * matrices, matrices)],
+            local_sem.at[0],
+        )
+        for j in range(block_cols)
+    ] + [
+        pltpu.make_async_copy(old_hbm, roots.at[pl.ds(0, capacity)], local_sem.at[1]),
+        pltpu.make_async_copy(fresh_hbm, roots.at[pl.ds(capacity, 1)], local_sem.at[2]),
+        pltpu.make_async_copy(left_hbm, left, local_sem.at[3]),
+        pltpu.make_async_copy(right_hbm, right, local_sem.at[4]),
+    ]
+    for load in loads:
+        load.start()
+
+    barrier = pltpu.get_barrier_semaphore()
+
+    @pl.loop(1, grp_count)
+    def _(k):
+        pl.semaphore_signal(barrier, 1, device_id=(f, along(k)), device_id_type=MESH)
+
+    @pl.loop(1, fsdp_count)
+    def _(k):
+        pl.semaphore_signal(barrier, 1, device_id=(across(k), g), device_id_type=MESH)
+
+    fill_table(
+        owner_row[...], refresh_row[...], table, g, fsdp_count, grp_count, capacity, block_cols, lengths
+    )
+    to_scalars = pltpu.make_async_copy(table, lookup, local_sem.at[5])
+    to_scalars.start()
+    pltpu.make_async_copy(grad, grad, local_sem.at[0]).wait()
+    to_scalars.wait()
+
+    def remote(source, target, phase, c, device):
+        return pltpu.make_async_remote_copy(
+            src_ref=source,
+            dst_ref=target,
+            send_sem=send_sem.at[phase, c],
+            recv_sem=recv_sem.at[phase, c],
+            device_id=device,
+            device_id_type=MESH,
+        )
+
+    def stays(source, target, phase, c):
+        return pltpu.make_async_copy(source, target, self_sem.at[phase, c])
+
+    def finish(source, target, phase, c):
+        everything = remote(source, target, phase, c, (f, g))
+        everything.wait_send()
+        everything.wait_recv()
+
+    def send_lists(source, target, length, phase, c):
+        spot = target.at[pl.ds(g * length, length)]
+        for k in both_ways(grp_count):
+            remote(source.at[c, along(k)], spot, phase, c, (f, along(k))).start()
+        stays(source.at[c, g], spot, phase, c).start()
+
+    def await_lists(source, target, length, phase, c):
+        stays(source.at[c, 0], target.at[pl.ds(0, length)], phase, c).wait()
+        others = grp_count - 1
+        finish(source.at[c, pl.ds(0, others)], target.at[pl.ds(0, others * length)], phase, c)
+
+    def send_bands(source_of, target, phase, c):
+        def send(k):
+            remote(source_of(across(k)), target, phase, c, (across(k), g)).start()
+
+        send(fsdp_count // 2)
+
+        @pl.loop(1, fsdp_count // 2)
+        def _(k):
+            send(k)
+            send(fsdp_count - k)
+
+        stays(source_of(f), target, phase, c).start()
+
+    def await_bands(buffer, roles, phase, c):
+        own = buffer.at[pl.ds(0, roles)]
+        stays(own, own, phase, c).wait()
+        others = buffer.at[pl.ds(0, (fsdp_count - 1) * roles)]
+        finish(others, others, phase, c)
+
+    def lanes(c):
+        return pl.ds(c * width, width)
+
+    def band(to):
+        return pl.ds(pl.multiple_of(to * plane_rows, 16), plane_rows)
+
+    def gather_rows(chunks):
+        @pl.loop(0, grp_count)
+        def _(to):
+            @pl.loop(0, in_length, unroll=4)
+            def _(i):
+                both = grad[lookup[0, to * in_length + i]]
+                for c in chunks:
+                    out1[c, to, i] = both[:, c * width : (c + 1) * width]
+
+    def spread_rows(c):
+        await_lists(out1, in1[c], in_length, 0, c)
+
+        def collect(to):
+            for role in range(roles_in):
+                i = lookup[1, to * roles_in + role]
+                tiles = [in1[c][source * in_length + i] for source in range(grp_count)]
+                out2[c, to * roles_in + role] = jnp.concatenate(tiles, axis=0)
+            return out2.at[c, pl.ds(to * roles_in, roles_in)]
+
+        send_bands(collect, pieces.at[:, band(f), lanes(c)], 1, c)
+
+    def apply_roots(role, h):
+        some = pl.ds(h * (block // 2), block // 2)
+        applied = jnp.dot(roots[role, 0], pieces[role, :, some], preferred_element_type=jnp.float32)
+        total = jnp.dot(applied.astype(jnp.bfloat16), roots[role, 1, some, :], preferred_element_type=jnp.float32)
+        if h == 0:
+            product[role] = total
+        else:
+            total = product[role] + total
+            wide = pieces[role].astype(jnp.float32)
+            count = 1.0 / (block * block)
+            scale = jnp.sqrt(jnp.sum(wide * wide, keepdims=True) * count + epsilon) * lax.rsqrt(
+                jnp.sum(total * total, keepdims=True) * count + epsilon
+            )
+            shaped[role] = (total * scale).astype(jnp.bfloat16)
+
+    def hop(c, to):
+        return remote(shaped.at[capacity, :, lanes(c)], back.at[c], 4, c, (f, to))
+
+    def mine(slot):
+        return owner_row[...] == (f * grp_count + g) * capacity + slot
+
+    def send_back(c):
+        hop(c, along(1)).wait_recv()
+        for slot in range(capacity):
+            renewed = jnp.sum(jnp.where(mine(slot), refresh_row[...], 0), axis=1, keepdims=True) == 1
+            settled[slot, :, lanes(c)] = jnp.where(renewed, back[c], shaped[slot, :, lanes(c)])
+        target = in3[c].at[pl.ds(f * capacity, capacity)]
+        send_bands(lambda to: settled.at[:, band(to), lanes(c)], target, 2, c)
+
+    def return_rows(c):
+        await_bands(in3[c], capacity, 2, c)
+
+        @pl.loop(0, out_length, unroll=2)
+        def _(i):
+            tile = in3[c][lookup[3, i]]
+            for to in range(grp_count):
+                out4[c, to, i] = tile[to * rows : (to + 1) * rows]
+
+        send_lists(out4, in4[c], out_length, 3, c)
+
+    def update_statistics(slot):
+        piece = pieces[slot]
+        held = jnp.sum(mine(slot).astype(jnp.int32), axis=1, keepdims=True) > 0
+        keep = jnp.where(held, jnp.float32(decay_rate), jnp.float32(1.0))
+        add = jnp.where(held, jnp.float32(1.0 - decay_rate), jnp.float32(0.0))
+        outer = lax.dot_general(piece, piece, (((1,), (1,)), ((), ())), preferred_element_type=jnp.float32)
+        left[slot] = keep * left[slot] + add * outer
+        inner = lax.dot_general(piece, piece, (((0,), (0,)), ((), ())), preferred_element_type=jnp.float32)
+        right[slot] = keep * right[slot] + add * inner
+
+    gather_rows([0])
+    pl.semaphore_wait(barrier, grp_count - 1 + fsdp_count - 1)
+    send_lists(out1, in1[0], in_length, 0, 0)
+    gather_rows(range(1, CHUNKS))
+    for c in range(1, CHUNKS):
+        send_lists(out1, in1[c], in_length, 0, c)
+
+    for c in range(CHUNKS):
+        spread_rows(c)
+    loads[-4].wait()
+    loads[-3].wait()
+    for c in range(CHUNKS):
+        await_bands(out2.at[c], roles_in, 1, c)
+        if c == CHUNKS // 2 - 1:
+            pl.loop(0, roles_in)(lambda role: apply_roots(role, 0))
+    pl.loop(capacity, roles_in)(lambda role: apply_roots(role, 1))
+    for c in range(CHUNKS):
+        hop(c, along(1)).start()
+    pl.loop(0, capacity)(lambda role: apply_roots(role, 1))
+    send_back(0)
+    send_back(1)
+    for c in range(2, CHUNKS):
+        return_rows(c - 2)
+        send_back(c)
+    loads[-2].wait()
+    loads[-1].wait()
+    pl.loop(0, 1)(update_statistics)
+    return_rows(CHUNKS - 2)
+    return_rows(CHUNKS - 1)
+    pl.loop(1, capacity)(update_statistics)
+    stores = [
+        pltpu.make_async_copy(left, new_left_hbm, local_sem.at[5]),
+        pltpu.make_async_copy(right, new_right_hbm, local_sem.at[6]),
+    ]
+    for store in stores:
+        store.start()
+
+    for c in range(CHUNKS):
+        hop(c, along(1)).wait_send()
+        await_lists(out4, in4[c], out_length, 3, c)
+
+        @pl.loop(0, matrices)
+        def _(m):
+            for j in range(block_cols):
+                column = j * block + c * width
+                update[m, :, pl.ds(column, width)] = in4[c][lookup[2, m * block_cols + j]]
+
+    for store in stores:
+        store.wait()
+
+
+def listed_plan(level, owner, refresh, grad, stats_left, stats_right, old_roots, fresh_roots):
+    matrices, rows, total_width = grad.shape
+    capacity, block = stats_left.shape[0], stats_left.shape[1]
+    fsdp_count, grp_count = lax.axis_size("fsdp"), lax.axis_size("grp")
+    sizes = (fsdp_count, grp_count, capacity, rows, block, total_width // block, matrices)
+    width, plane_rows = block // CHUNKS, grp_count * rows
+    bf16, f32 = jnp.bfloat16, jnp.float32
+    roles = capacity + 1
+    in_length, out_length = LISTS[level]
+    vmem, hbm = pl.BlockSpec(memory_space=pltpu.VMEM), pl.BlockSpec(memory_space=pl.ANY)
+    return pl.pallas_call(
+        functools.partial(step_kernel, sizes, LISTS[level]),
+        out_shape=(
+            jax.ShapeDtypeStruct(stats_left.shape, f32),
+            jax.ShapeDtypeStruct(stats_right.shape, f32),
+            jax.ShapeDtypeStruct(grad.shape, bf16),
+        ),
+        in_specs=[vmem] * 2 + [hbm] * 5,
+        out_specs=(hbm, hbm, vmem),
+        scratch_shapes=[
+            pltpu.VMEM((matrices * (total_width // block), rows, block), bf16),
+            pltpu.VMEM((CHUNKS, grp_count, in_length, rows, width), bf16),
+            [pltpu.VMEM((grp_count * in_length, rows, width), bf16)] * CHUNKS,
+            pltpu.VMEM((CHUNKS, fsdp_count * roles, plane_rows, width), bf16),
+            pltpu.VMEM((roles, block, block), bf16),
+            pltpu.VMEM((roles, block, block), f32),
+            pltpu.VMEM((roles, block, block), bf16),
+            pltpu.VMEM((CHUNKS, block, width), bf16),
+            pltpu.VMEM((capacity, block, block), bf16),
+            [pltpu.VMEM((fsdp_count * capacity, plane_rows, width), bf16)] * CHUNKS,
+            pltpu.VMEM((CHUNKS, grp_count, out_length, rows, width), bf16),
+            [pltpu.VMEM((grp_count * out_length, rows, width), bf16)] * CHUNKS,
+            pltpu.VMEM((roles, 2, block, block), bf16),
+            pltpu.VMEM(stats_left.shape, f32),
+            pltpu.VMEM(stats_right.shape, f32),
+            pltpu.VMEM((8, 512), jnp.int32),
+            pltpu.SMEM((8, 512), jnp.int32),
+            pltpu.SemaphoreType.DMA((7,)),
+            pltpu.SemaphoreType.DMA((4, CHUNKS)),
+            pltpu.SemaphoreType.DMA((5, CHUNKS)),
+            pltpu.SemaphoreType.DMA((5, CHUNKS)),
+        ],
+        compiler_params=pltpu.CompilerParams(
+            collective_id=1 + level, has_side_effects=True, vmem_limit_bytes=28 * 1024 * 1024
+        ),
+        name="listed_step",
+    )(owner[None], refresh[None], grad, stats_left, stats_right, old_roots, fresh_roots)
+
+
+def hand_over_kernel(pieces, *refs):
+    count = len(refs) // 3
+    into, out_of = refs[-2:]
+    moves = []
+    for n in range(count):
+        source, target, room = refs[n], refs[count + n], refs[2 * count + n]
+        share = source.shape[0] // pieces
+        for p in range(pieces):
+            some, i = pl.ds(p * share, share), n * pieces + p
+            moves.append(
+                (
+                    pltpu.make_async_copy(source.at[some], room.at[some], into.at[i]),
+                    pltpu.make_async_copy(room.at[some], target.at[some], out_of.at[i]),
+                )
+            )
+    for fetch, _ in moves:
+        fetch.start()
+    for fetch, store in moves:
+        fetch.wait()
+        store.start()
+    for _, store in moves:
+        store.wait()
+
+
+def hand_over(*arrays):
+    pieces = 2
+    hbm = pl.BlockSpec(memory_space=pl.ANY)
+    sems = pltpu.SemaphoreType.DMA((len(arrays) * pieces,))
+    return pl.pallas_call(
+        functools.partial(hand_over_kernel, pieces),
+        out_shape=[jax.ShapeDtypeStruct(a.shape, a.dtype) for a in arrays],
+        in_specs=[hbm] * len(arrays),
+        out_specs=[hbm] * len(arrays),
+        scratch_shapes=[pltpu.VMEM(a.shape, a.dtype) for a in arrays] + [sems, sems],
+        compiler_params=pltpu.CompilerParams(vmem_limit_bytes=16 * 1024 * 1024),
+        name="hand_over",
+    )(*arrays)
+
+
+def local(*arrays):
+    grad, owner, refresh, *held = arrays
+    branch = too_short(owner, refresh, lax.axis_size("grp"), held[0].shape[0])
+    plans = [
+        lambda level=level: listed_plan(level, owner, refresh, grad, *held) for level in range(len(LISTS))
+    ]
+    return tuple(hand_over(*lax.switch(branch, [*plans, lambda: dense_plan(*arrays)])))
+
+
 def solution(mesh):
     return jax.shard_map(
         local,

time: 168 us -> 77.3 us (0.46)
  Pallas kernels: 0 us -> 72.6 us
  waiting for transfers between devices: 67.3 us -> 0 us
  blocking collectives: 46.8 us -> 0 us
  local copies, waits for them, and re-layouts: 18.8 us -> 0 us
  starting transfers between devices: 14 us -> 0 us
  matrix products: 10.3 us -> 0 us
  other arithmetic: 9.93 us -> 2.22 us
    pallas_call x0 -> x2, Pallas kernels: none -> 72.6 us  [the longest x1 69.1 us: listed_plan(): pl.pallas_call(functools.partial(step_kernel, sizes, LISTS[level]), out_s...]
    all_to_all x2 -> x0, blocking collectives: 46.8 us -> none  [the longest x1 25.3 us: local(): lax.all_to_all(outbound, 'fsdp', split_axis=1, concat_axis=1, tiled=True)]
    ppermute x1 -> x0, waiting for transfers between devices: 46.5 us -> none  [shifted(): return lax.ppermute(block, axis, route)]
    all_to_all x2 -> x0, waiting for transfers between devices: 20.7 us -> none  [the longest x1 20.7 us: local(): lax.all_to_all(lax.all_to_all(outgoing, 'fsdp', split_axis=1, concat_axis...]
    all_to_all x2 -> x0, starting transfers between devices: 12.5 us -> none  [the longest x1 8.19 us: local(): lax.all_to_all(lax.all_to_all(outbound, 'fsdp', split_axis=1, concat_axis...]
    dot_general x3 -> x0, matrix products: 10.3 us -> none  [the longest x1 4.13 us: slot_work(): jnp.dot(left_applied, inverse_roots[1], preferred_element_type=jnp.float32)]
    gather x3 -> x0, local copies, waits for them, and re-layouts: 7.87 us -> none  [the longest x1 3.56 us: local(): local_blocks[local_index]]
    all_to_all x4 -> x0, local copies, waits for them, and re-layouts: 5.71 us -> none  [the longest x1 2 us: local(): lax.all_to_all(outgoing, 'fsdp', split_axis=1, concat_axis=1, tiled=True)]
  transfers between devices with their start and end apart: 3 -> 0, of which waited for: 2 -> 0; matrix products, arithmetic and copies ran while one was open for 7% -> 0% of each run, Pallas kernels for 0% -> 0%
where the time goes in v3:
time: 77.3 us; the launch traced here: 77.2 us
  Pallas kernels  72.6 us (94%)
  other arithmetic  2.22 us (3%)
  between operations  2.12 us (3%)
    pallas_call x1, Pallas kernels, listed_plan(): pl.pallas_call(functools.partial(step_kernel, sizes, LISTS[level]), out_s...  69.1 us
    pallas_call x1, Pallas kernels, hand_over(): pl.pallas_call(functools.partial(hand_over_kernel, pieces), out_shape=[ja...  3.47 us

profile of v3, /device:TPU:1, one launch (start us, length us, event | category | flops | bytes accessed | tf_op | source)
XLA Modules:
  0.0 77.2 jit_solution(16631431853039895240)
XLA Ops:
  0.6 0.7 shift-right-arithmetic_and_fusion
  1.3 0.9 %fusion.6 = (s32[8]{0:T(128)S(1)}, s32[8]{0:T(128)S(1)}) fusion(s32[224]{0:T(256)} %param.14, s32[224]{0:T(256)S(1)} %shift-right-arithmetic_and_fusion, s32[8]{0:T(128)} %constant.161), kind=kLoop, calls=%fused_computation.50 | loop fusion | flops 12528 | bytes 1888 | tf_op jit(solution)/shard_map/reduce_sum | solution.py:127
  2.2 0.6 maximum_reduce_fusion
  4.2 69.3 %conditional.1 = ((f32[2,512,512]{2,1,0:T(8,128)}, f32[2,512,512]{2,1,0:T(8,128)}, bf16[16,2,7168]{2,1,0:T(2,128)(2,1)})) conditional(s32[]{:T(128)} %clamp.3, (s32[224]{0:T(256)}, s32[224]{0:T(256)}, bf16[16,2,7168]{2,1,0:T(2,128)(2,1)}, f32[2,512,512]{2,1,0:T(8,128)}, f32[2,512,512]{2,1,0:T(8,128)}, ...), branch_computations={%region_4.5_spmd, %region_5.6_spmd, %region_6.13_spmd} | conditional | flops 2158039552 | bytes 88810224 | solution.py:542
  4.2 69.1 %listed_step.2 = (f32[2,512,512]{2,1,0:T(8,128)}, f32[2,512,512]{2,1,0:T(8,128)}, bf16[16,2,7168]{2,1,0:T(2,128)(2,1)}) custom-call(s32[1,224]{1,0:T(1,128)} %bitcast.37, s32[1,224]{1,0:T(1,128)} %bitcast.43, bf16[16,2,7168]{2,1,0:T(2,128)(2,1)} %get-tuple-element.44.grad_hbm, f32[2,512,512]{2,1,0:T(8,128)} %get-tuple-element.45.left_hbm, ...), custom_call_target="tpu_custom_call" | custom-call | tf_op jit(solution)/shard_map/cond/branch_0_fun/listed_step/pallas_call | solution.py:458
  73.5 3.5 %hand_over.1 = (f32[2,512,512]{2,1,0:T(8,128)}, f32[2,512,512]{2,1,0:T(8,128)}, bf16[16,2,7168]{2,1,0:T(2,128)(2,1)}) custom-call(f32[2,512,512]{2,1,0:T(8,128)} %get-tuple-element.69.refs_0_, f32[2,512,512]{2,1,0:T(8,128)} %get-tuple-element.70.refs_1_, bf16[16,2,7168]{2,1,0:T(2,128)(2,1)} %get-tuple-element.157.refs_2_), custom_call_target="tpu_custom_call" | custom-call | tf_op jit(solution)/shard_map/hand_over/pallas_call | solution.py:525

commit v4 on v3

--- a/solution.py
+++ b/solution.py
@@ -12,7 +12,7 @@
 epsilon = 1e-06
 
 CHUNKS = 4
-LISTS = ((48, 38), (64, 56))
+LISTS = ((48, 38), (54, 44))
 
 MESH = pl.DeviceIdType.MESH
 

time: 77.3 us -> 77.3 us (level)
  no operation moved by 1% of the time
where the time goes in v4:
time: 77.3 us; the launch traced here: 77.2 us
  Pallas kernels  72.6 us (94%)
  other arithmetic  2.22 us (3%)
  between operations  2.12 us (3%)
    pallas_call x1, Pallas kernels, listed_plan(): pl.pallas_call(functools.partial(step_kernel, sizes, LISTS[level]), out_s...  69.1 us
    pallas_call x1, Pallas kernels, hand_over(): pl.pallas_call(functools.partial(hand_over_kernel, pieces), out_shape=[ja...  3.47 us

profile of v4, /device:TPU:1, one launch (start us, length us, event | category | flops | bytes accessed | tf_op | source)
XLA Modules:
  0.0 77.2 jit_solution(12959159064186215816)
XLA Ops:
  0.6 0.7 shift-right-arithmetic_and_fusion
  1.3 0.9 %fusion.6 = (s32[8]{0:T(128)S(1)}, s32[8]{0:T(128)S(1)}) fusion(s32[224]{0:T(256)} %param.14, s32[224]{0:T(256)S(1)} %shift-right-arithmetic_and_fusion, s32[8]{0:T(128)} %constant.161), kind=kLoop, calls=%fused_computation.50 | loop fusion | flops 12528 | bytes 1888 | tf_op jit(solution)/shard_map/reduce_sum | solution.py:127
  2.2 0.6 maximum_reduce_fusion
  4.2 69.3 %conditional.1 = ((f32[2,512,512]{2,1,0:T(8,128)}, f32[2,512,512]{2,1,0:T(8,128)}, bf16[16,2,7168]{2,1,0:T(2,128)(2,1)})) conditional(s32[]{:T(128)} %clamp.3, (s32[224]{0:T(256)}, s32[224]{0:T(256)}, bf16[16,2,7168]{2,1,0:T(2,128)(2,1)}, f32[2,512,512]{2,1,0:T(8,128)}, f32[2,512,512]{2,1,0:T(8,128)}, ...), branch_computations={%region_4.5_spmd, %region_5.6_spmd, %region_6.13_spmd} | conditional | flops 2158039552 | bytes 88810224 | solution.py:542
  4.2 69.1 %listed_step.2 = (f32[2,512,512]{2,1,0:T(8,128)}, f32[2,512,512]{2,1,0:T(8,128)}, bf16[16,2,7168]{2,1,0:T(2,128)(2,1)}) custom-call(s32[1,224]{1,0:T(1,128)} %bitcast.37, s32[1,224]{1,0:T(1,128)} %bitcast.43, bf16[16,2,7168]{2,1,0:T(2,128)(2,1)} %get-tuple-element.44.grad_hbm, f32[2,512,512]{2,1,0:T(8,128)} %get-tuple-element.45.left_hbm, ...), custom_call_target="tpu_custom_call" | custom-call | tf_op jit(solution)/shard_map/cond/branch_0_fun/listed_step/pallas_call | solution.py:458
  73.5 3.5 %hand_over.1 = (f32[2,512,512]{2,1,0:T(8,128)}, f32[2,512,512]{2,1,0:T(8,128)}, bf16[16,2,7168]{2,1,0:T(2,128)(2,1)}) custom-call(f32[2,512,512]{2,1,0:T(8,128)} %get-tuple-element.69.refs_0_, f32[2,512,512]{2,1,0:T(8,128)} %get-tuple-element.70.refs_1_, bf16[16,2,7168]{2,1,0:T(2,128)(2,1)} %get-tuple-element.157.refs_2_), custom_call_target="tpu_custom_call" | custom-call | tf_op jit(solution)/shard_map/hand_over/pallas_call | solution.py:525
